TPU v7x, 32 devices: a whole 2x2x4 slice. The times are simulated.
32 devices in a mesh: graph: 4 (over z), index: 8 (over y, x, core).
Axes of the slice: x: 2, y: 2, z: 4, core: 2. Of those that a mesh axis runs over, the one named last changes fastest.
Arguments:
- features: bfloat16 [8192, 1024], P(('graph', 'index')), may hold values from -6 to 6
- q_weight: bfloat16 [1024, 1024], replicated, may hold values from -0.1875 to 0.1875
- q_bias: float32 [1024], replicated, may hold values from -3 to 3
- w_self: bfloat16 [1024, 1024], replicated, may hold values from -0.125 to 0.125
- w_neigh: bfloat16 [1024, 1024], replicated, may hold values from -0.125 to 0.125
- z_bias: float32 [1024], replicated, may hold values from -3 to 3
- centroids: bfloat16 [2048, 1024], P('index'), may hold values from -0.1875 to 0.1875
- requests: int32 [32, 8, 16], P(('graph', 'index')), may hold values from 0 to 255, as said below
- slots: int32 [8192, 50], P(('graph', 'index')), may hold values from 0 to 127
- importance: float32 [8192, 50], P(('graph', 'index')), may hold values from 0.1 to 10
- labels: int32 [8192, 1], P(('graph', 'index')), may hold values from 0 to 7; in each aligned block of 256 rows (0 to 255, 256 to 511, ...) at most 64 rows name the same one
Outputs:
- scores: bfloat16 [8192, 256], P(('graph', 'index'))
Inputs may be any that keep to these rules, and one draw needn't show every extreme that they name: `requests`: the 16 rows that a device asks of one device are distinct. `labels`: the rows of one device carry any one label at most 64 times.
All inputs are finite; a program needn't handle non-finite values.
Results may differ from a plain program's by a relative error of at most 0.0051.
Values may be sent and summed in bfloat16 or wider, within the bound.
A program may use at most 64 MiB of HBM per device.

v0:
```python
import jax
import jax.numpy as jnp
from jax import lax
from jax.sharding import PartitionSpec as P


def place_rows(label_rows, peer_count, owner_slots):
    hits = (label_rows[:, None] == jnp.arange(peer_count, dtype=jnp.int32)[None, :]).astype(
        jnp.int32
    )
    ranks = jnp.sum(hits * (jnp.cumsum(hits, axis=0) - 1), axis=1)
    return label_rows * owner_slots + ranks


def body(
    features,
    q_weight,
    q_bias,
    w_self,
    w_neigh,
    z_bias,
    centroids,
    requests,
    slots,
    importance,
    labels,
):
    row_count = features.shape[0]
    width = features.shape[1]
    peer_count = lax.axis_size("index")
    owner_slots = max(2 * row_count // peer_count, 2)
    fetch_slots = requests.shape[2]
    slot_count = peer_count * fetch_slots
    cent_count = centroids.shape[0]
    messages = jax.nn.relu(
        jnp.dot(features, q_weight, preferred_element_type=jnp.float32) + q_bias
    ).astype(jnp.bfloat16)
    weights_norm = importance / jnp.sum(importance, axis=1, keepdims=True)
    slot_ids = jnp.arange(slot_count, dtype=jnp.int32)
    mixing = jnp.sum(
        jnp.where(slots[:, :, None] == slot_ids[None, None, :], weights_norm[:, :, None], 0.0),
        axis=1,
    ).astype(jnp.bfloat16)
    asked_rows = requests[0]
    columns = (jnp.arange(peer_count, dtype=jnp.int32)[:, None] * row_count + asked_rows).reshape(
        -1
    )
    shard_rows = lax.all_gather(messages, "index", axis=0, tiled=True)
    targets = jnp.arange(shard_rows.shape[0], dtype=jnp.int32)
    select = (columns[:, None] == targets[None, :]).astype(jnp.bfloat16)
    local_mix = jnp.dot(mixing, select, preferred_element_type=jnp.float32).astype(jnp.bfloat16)
    pooled = jnp.dot(local_mix, shard_rows, preferred_element_type=jnp.float32).astype(jnp.bfloat16)
    hidden = jax.nn.relu(
        jnp.dot(features, w_self, preferred_element_type=jnp.float32)
        + jnp.dot(pooled, w_neigh, preferred_element_type=jnp.float32)
        + z_bias
    )
    normed = (hidden * lax.rsqrt(jnp.mean(hidden * hidden, axis=1, keepdims=True) + 1e-06)).astype(
        jnp.bfloat16
    )
    positions = place_rows(labels[:, 0], peer_count, owner_slots)
    outgoing = jnp.zeros((peer_count * owner_slots, width), jnp.bfloat16).at[positions].set(normed)
    outgoing = outgoing.reshape(peer_count, owner_slots, width)
    arrived = lax.all_to_all(outgoing, "index", split_axis=0, concat_axis=0, tiled=True)
    flat_rows = arrived.reshape(-1, width)
    raw_scores = lax.dot_general(
        flat_rows, centroids, (((1,), (1,)), ((), ())), preferred_element_type=jnp.float32
    ).astype(jnp.bfloat16)
    returned = lax.all_to_all(
        raw_scores.reshape(peer_count, arrived.shape[1], cent_count),
        "index",
        split_axis=0,
        concat_axis=0,
        tiled=True,
    )
    return jnp.take(returned.reshape(peer_count * owner_slots, cent_count), positions, axis=0)


def solution(mesh):
    return jax.shard_map(
        body,
        mesh=mesh,
        in_specs=(
            P(("graph", "index"), None),
            P(),
            P(),
            P(),
            P(),
            P(),
            P("index", None),
            P(("graph", "index"), None, None),
            P(("graph", "index"), None),
            P(("graph", "index"), None),
            P(("graph", "index"), None),
        ),
        out_specs=P(("graph", "index"), None),
        check_vma=False,
    )
```

profile of v0, /device:TPU:0, one launch (start us, length us, event | category | flops | bytes accessed | tf_op | source)
XLA Modules:
  0.0 97.8 jit_solution(9600827252645665040)
XLA Ops:
  6.5 0.0 copy-start
  6.5 0.0 copy-start.4
  6.5 0.0 copy-start.5
  6.5 0.0 copy-start.1
  6.5 0.0 copy-start.2
  6.5 0.0 all-gather.2.cloned.1.call-start
  6.6 3.3 %fusion.4 = bf16[256,1024]{1,0:T(8,128)(2,1)} fusion(bf16[256,1024]{1,0:T(8,128)(2,1)} %param.11, bf16[1024,1024]{1,0:T(8,128)(2,1)} %param.12, f32[1024]{0:T(1024)} %param.13), kind=kOutput, calls=%fused_computation.11 | convolution fusion | flops 537657344 | bytes 3149824 | tf_op jit(solution)/shard_map/dot_general | solution.py:36
  9.9 0.0 all-gather.2.cloned.1.call-update
  9.9 0.0 copy-done.4
  10.0 0.6 reduce-window.6
  10.5 0.2 slice_reduce_fusion
  10.8 0.1 add.67
  10.9 0.1 add.68
  11.0 0.0 copy-done.5
  11.0 0.1 squeeze.4
  11.0 0.0 copy-done.1
  11.1 0.1 fusion.13
  11.2 0.0 copy-done.2
  11.2 5.6 %select_reduce_fusion = bf16[256,128]{1,0:T(8,128)(2,1)S(1)} fusion(f32[256,50]{0,1:T(8,128)S(1)} %broadcast_divide_fusion, s32[256,50]{0,1:T(8,128)S(1)} %copy-done.2), kind=kLoop, calls=%fused_computation.2 | loop fusion | flops 4882432 | bytes 167936 | tf_op jit(solution)/shard_map/reduce_sum | solution.py:40
  16.8 2.5 %fusion.15 = f32[256,1024]{1,0:T(8,128)S(1)} fusion(bf16[256,1024]{1,0:T(8,128)(2,1)} %param.11, bf16[1024,1024]{1,0:T(8,128)(2,1)} %param.14), kind=kOutput, calls=%fused_computation.35 | convolution fusion | flops 536870912 | bytes 3670016 | tf_op jit(solution)/shard_map/dot_general | solution.py:54
  19.3 0.0 copy-start.3
  19.3 30.2 %all-gather.2.cloned.1.call-done = bf16[2048,1024]{1,0:T(8,128)(2,1)} async-done(((bf16[256,1024]{1,0:T(8,128)(2,1)}), bf16[2048,1024]{1,0:T(8,128)(2,1)}) %all-gather.2.cloned.1.call-update) | async-done | bytes 4194320 | tf_op jit(solution)/shard_map/all_gather | solution.py:48
  49.5 4.6 %fusion.5 = bf16[256,1024]{1,0:T(8,128)(2,1)} fusion(bf16[2048,1024]{1,0:T(8,128)(2,1)} %all-gather.2.cloned.1.call-done, s32[128]{0:T(128)S(1)} %add.69, bf16[256,128]{1,0:T(8,128)(2,1)S(1)} %select_reduce_fusion), kind=kOutput, calls=%fused_computation.12 | convolution fusion | flops 1209008128 | bytes 4784640 | tf_op jit(solution)/shard_map/dot_general | solution.py:52
  54.1 0.0 copy-done
  54.1 0.0 copy-done.3
  54.1 2.8 %multiply_reduce_fusion = (f32[256]{0:T(256)S(1)}, f32[256,1024]{1,0:T(8,128)}) fusion(f32[1024]{0:T(1024)S(1)} %copy-done.3, f32[256,1024]{1,0:T(8,128)S(1)} %fusion.15, bf16[256,1024]{1,0:T(8,128)(2,1)} %fusion.5, bf16[1024,1024]{1,0:T(8,128)(2,1)S(1)} %copy-done), kind=kOutput, calls=%fused_computation.15 | convolution fusion | flops 538181376 | bytes 4723712 | tf_op jit(solution)/shard_map/dot_general | solution.py:55
  56.9 2.7 %scatter_custom_fusion = bf16[512,1024]{1,0:T(8,128)(2,1)S(1)} fusion(s32[256]{0:T(256)S(1)} %bitcast.29, f32[256,1024]{1,0:T(8,128)} %get-tuple-element.8, f32[256]{0:T(256)S(1)} %add_rsqrt_fusion, bf16[]{:T(256)} %constant.36.clone.1), kind=kCustom, calls=%fused_computation.17 | custom fusion | flops 524288 | bytes 2098178 | tf_op jit(solution)/shard_map/scatter | solution.py:62
  59.6 0.0 copy-start.6
  59.6 18.0 %all_to_all.10 = bf16[8,64,1024]{2,1,0:T(8,128)(2,1)S(1)} all-to-all(bf16[8,64,1024]{2,1,0:T(8,128)(2,1)S(1)} %bitcast.25), channel_id=1, replica_groups=mesh['graph'=4,'index'=8] {'index'}, dimensions={0} | all-to-all | bytes 2097152 | tf_op jit(solution)/shard_map/all_to_all | solution.py:64
  77.6 0.0 copy-done.6
  77.6 1.2 %convolution_convert_fusion.1 = bf16[512,256]{1,0:T(8,128)(2,1)} fusion(bf16[512,1024]{1,0:T(8,128)(2,1)S(1)} %bitcast.26, bf16[256,1024]{1,0:T(8,128)(2,1)S(1)} %copy-done.6), kind=kOutput, calls=%fused_computation.13 | convolution fusion | flops 268566528 | bytes 1835008 | tf_op jit(solution)/shard_map/dot_general | solution.py:66
  78.8 3.4 %all-to-all-start.1 = ((bf16[8,64,256]{2,1,0:T(8,128)(2,1)}), bf16[8,64,256]{2,1,0:T(8,128)(2,1)S(1)}, u32[]{:S(2)}, u32[]{:S(2)}) async-start(bf16[8,64,256]{2,1,0:T(8,128)(2,1)} %bitcast.8), calls=%async_computation.1 | async-start | bytes 524288 | tf_op jit(solution)/shard_map/all_to_all | solution.py:69
  82.2 6.9 %all-to-all-done.1 = bf16[8,64,256]{2,1,0:T(8,128)(2,1)S(1)} async-done(((bf16[8,64,256]{2,1,0:T(8,128)(2,1)}), bf16[8,64,256]{2,1,0:T(8,128)(2,1)S(1)}, u32[]{:S(2)}, u32[]{:S(2)}) %all-to-all-start.1) | async-done | bytes 262176 | tf_op jit(solution)/shard_map/all_to_all | solution.py:69
  89.1 1.2 %gather_fusion = bf16[256,256]{1,0:T(8,128)(2,1)S(1)} fusion(bf16[512,256]{1,0:T(8,128)(2,1)S(1)} %bitcast.24, s32[1024]{0:T(1024)S(1)} %pad_clamp_fusion), kind=kCustom, calls=%fused_computation | custom fusion | bytes 263168 | tf_op jit(solution)/shard_map/jit(_take)/gather | solution.py:76
  90.2 0.8 broadcast_select_fusion
  (10 shorter events, 0.1 us)
Async XLA Ops:
  6.5 47.6 %copy-start = (bf16[1024,1024]{1,0:T(8,128)(2,1)S(1)}, bf16[1024,1024]{1,0:T(8,128)(2,1)}, u32[]{:S(2)}) copy-start(bf16[1024,1024]{1,0:T(8,128)(2,1)} %param.15) | copy-start | bytes 6291460
  6.5 3.4 %copy-start.4 = (s32[256,1]{0,1:T(1,128)S(1)}, s32[256,1]{0,1:T(1,128)}, u32[]{:S(2)}) copy-start(s32[256,1]{0,1:T(1,128)} %param.21) | copy-start | bytes 3076
  6.5 4.4 %copy-start.5 = (s32[1,8,16]{2,1,0:T(8,128)S(1)}, s32[1,8,16]{2,1,0:T(8,128)}, u32[]{:S(2)}) copy-start(s32[1,8,16]{2,1,0:T(8,128)} %param.18) | copy-start | bytes 1540
  6.5 4.5 %copy-start.1 = (f32[256,50]{0,1:T(8,128)S(1)}, f32[256,50]{0,1:T(8,128)}, u32[]{:S(2)}) copy-start(f32[256,50]{0,1:T(8,128)} %param.20) | copy-start | bytes 153604
  6.5 4.7 %copy-start.2 = (s32[256,50]{0,1:T(8,128)S(1)}, s32[256,50]{0,1:T(8,128)}, u32[]{:S(2)}) copy-start(s32[256,50]{0,1:T(8,128)} %param.19) | copy-start | bytes 153604
  6.5 43.0 %all-gather.2.cloned.1.call-start = ((), (), s32[]{:S(2)}) async-start(), calls=%async_computation.2 | async-start | bytes 4718592 | tf_op jit(solution)/shard_map/all_gather | solution.py:48
  19.3 34.8 %copy-start.3 = (f32[1024]{0:T(1024)S(1)}, f32[1024]{0:T(1024)}, u32[]{:S(2)}) copy-start(f32[1024]{0:T(1024)} %param.16) | copy-start | bytes 12292
  59.6 18.0 %copy-start.6 = (bf16[256,1024]{1,0:T(8,128)(2,1)S(1)}, bf16[256,1024]{1,0:T(8,128)(2,1)}, u32[]{:S(2)}) copy-start(bf16[256,1024]{1,0:T(8,128)(2,1)} %param.17) | copy-start | bytes 1572868
  78.8 10.3 %all-to-all-start.1 = ((bf16[8,64,256]{2,1,0:T(8,128)(2,1)}), bf16[8,64,256]{2,1,0:T(8,128)(2,1)S(1)}, u32[]{:S(2)}, u32[]{:S(2)}) async-start(bf16[8,64,256]{2,1,0:T(8,128)(2,1)} %bitcast.8), calls=%async_computation.1 | async-start | bytes 524288 | tf_op jit(solution)/shard_map/all_to_all | solution.py:69
Sparse Core Ops, SparseCore 0:
  10.1 39.4 all-gather.1
where the time goes:
time: 98.2 us; the launch traced here: 97.8 us
  waiting for transfers between devices  37.1 us (38%)
  blocking collectives  18 us (18%)
  matrix products  14.3 us (15%)
  between operations  13.5 us (14%)
  other arithmetic  9.79 us (10%)
  starting transfers between devices  3.45 us (4%)
  local copies, waits for them, and re-layouts  1.63 us (2%)
    all_gather x1, waiting for transfers between devices, body(): shard_rows = lax.all_gather(messages, 'index', axis=0, tiled=True)  30.2 us
    all_to_all x1, blocking collectives, body(): lax.all_to_all(outgoing, 'index', split_axis=0, concat_axis=0, tiled=True)  18 us
    all_to_all x1, waiting for transfers between devices, body(): lax.all_to_all(raw_scores.reshape(peer_count, arrived.shape[1], cent_coun...  6.85 us
    reduce_sum x1, other arithmetic, body(): jnp.sum(jnp.where(slots[:, :, None] == slot_ids[None, None, :], weights_n...  5.56 us
    dot_general x1, matrix products, body(): jnp.dot(local_mix, shard_rows, preferred_element_type=jnp.float32)  4.59 us
    all_to_all x1, starting transfers between devices, body(): lax.all_to_all(raw_scores.reshape(peer_count, arrived.shape[1], cent_coun...  3.41 us
    dot_general x1, matrix products, body(): jnp.dot(features, q_weight, preferred_element_type=jnp.float32) + q_bias  3.32 us
    dot_general x1, matrix products, body(): jnp.dot(pooled, w_neigh, preferred_element_type=jnp.float32)  2.77 us
  transfers between devices with their start and end apart: 2, of which 2 were waited for; matrix products, arithmetic and copies ran while one was open for 9% of the time, Pallas kernels for 0%

commit v1 on v0

v1 whole, which is shorter than its diff:
```python
import functools

import jax
import jax.numpy as jnp
from jax import lax
from jax.experimental import pallas as pl
from jax.experimental.pallas import tpu as pltpu
from jax.sharding import PartitionSpec as P

MESH = pl.DeviceIdType.MESH
LANES = 128
TILE = 256


def chip_bits(peers):
    return [1 << k for k in range(1, peers.bit_length() - 1)]


def even_offsets(peers):
    return sorted(range(2, peers, 2), key=lambda d: (bin(d).count("1"), d))


def kernel(
    graphs,
    peers,
    features_hbm,
    q_weight_hbm,
    q_bias_hbm,
    w_self_hbm,
    w_neigh_hbm,
    z_bias_hbm,
    centroids_hbm,
    requests_hbm,
    slots_hbm,
    importance_hbm,
    labels_hbm,
    out_ref,
    features,
    q_weight,
    q_bias,
    w_self,
    w_neigh,
    z_bias,
    shards,
    requests,
    slots,
    importance,
    labels,
    asked,
    rows_out,
    rows_in,
    mixing,
    pooled,
    hidden,
    squares,
    normed,
    total,
    load_sems,
    send_sems,
    main_sems,
    side_sems,
    asked_sems,
    rows_sems,
):
    graph = lax.axis_index("graph")
    me = lax.axis_index("index")
    row_count, width = features.shape
    cents = shards.shape[1]
    fetch = requests.shape[1]
    slot_count = peers * fetch
    bits = chip_bits(peers)

    def flip(value, bit):
        return value + bit * (1 - 2 * ((value // bit) % 2))

    def at_offset(offset):
        value = me
        bit = 1
        while bit < peers:
            if offset & bit:
                value = flip(value, bit)
            bit *= 2
        return value

    role = graph % 2
    across = flip(graph, 1)

    share = cents * 5 // 16 // 16 * 16
    common = cents - 2 * share
    share_a = (share // 2 + 15) // 16 * 16
    common_a = (common // 2 + 15) // 16 * 16

    def rows_of(part):
        start, size = {
            0: (role * share, share_a),
            1: (role * share + share_a, share - share_a),
            2: (2 * share, common_a),
            3: (2 * share + common_a, common - common_a),
            4: ((1 - role) * share, share_a),
            5: ((1 - role) * share + share_a, share - share_a),
        }[part]
        return pl.ds(start if isinstance(start, int) else pl.multiple_of(start, 16), size)

    loads = []
    for source, target in (
        (requests_hbm, requests),
        (features_hbm, features),
        (centroids_hbm, shards.at[me]),
        (slots_hbm, slots),
        (importance_hbm, importance),
        (w_self_hbm, w_self),
        (z_bias_hbm, z_bias),
        (q_weight_hbm, q_weight),
        (q_bias_hbm, q_bias),
        (w_neigh_hbm, w_neigh),
        (labels_hbm, labels),
    ):
        load = pltpu.make_async_copy(source, target, load_sems.at[len(loads)])
        load.start()
        loads.append(load)

    barrier = pltpu.get_barrier_semaphore()
    for offset in range(1, peers):
        pl.semaphore_signal(barrier, inc=1, device_id=(graph, at_offset(offset)), device_id_type=MESH)
    pl.semaphore_signal(barrier, inc=1, device_id=(across, me), device_id_type=MESH)
    pl.semaphore_wait(barrier, peers)

    sent = []

    def send(source, target, arrival, device):
        copy = pltpu.make_async_remote_copy(
            src_ref=source,
            dst_ref=target,
            send_sem=send_sems.at[len(sent)],
            recv_sem=arrival,
            device_id=device,
            device_id_type=MESH,
        )
        copy.start()
        sent.append(copy)

    def await_arrival(target, arrival):
        pltpu.make_async_remote_copy(
            src_ref=target,
            dst_ref=target,
            send_sem=send_sems.at[0],
            recv_sem=arrival,
            device_id=(graph, at_offset(1)),
            device_id_type=MESH,
        ).wait_recv()

    def part_ref(offset, part):
        return shards.at[at_offset(offset), rows_of(part)]

    def send_on(offset, part, bit):
        ref = part_ref(offset, part)
        send(ref, ref, main_sems.at[(offset | bit) // 2, part], (graph, flip(me, bit)))

    def relay(offset, part):
        ref = part_ref(offset, part)
        await_arrival(ref, main_sems.at[offset // 2, part])
        if part in (0, 2):
            for bit in bits:
                if bit > offset:
                    send_on(offset, part, bit)
        elif part in (1, 3):
            for bit in bits:
                if bit < (offset & -offset):
                    send_on(offset, part, bit)
        if part in (0, 1):
            send(ref, ref, main_sems.at[offset // 2, part + 4], (across, me))
        send(ref, ref, side_sems.at[offset // 2, part], (graph, flip(me, 1)))

    loads[0].wait()
    for offset in range(1, peers):
        peer = at_offset(offset)
        send(requests.at[peer], asked.at[me], asked_sems.at[offset], (graph, peer))
    asked[pl.ds(me, 1)] = requests[pl.ds(me, 1)]

    loads[2].wait()
    for part in (0, 1):
        for bit in bits:
            send_on(0, part, bit)
    send(shards.at[me], shards.at[me], side_sems.at[0, 0], (graph, flip(me, 1)))

    loads[1].wait()
    for offset in range(1, peers):
        await_arrival(asked.at[at_offset(offset)], asked_sems.at[offset])
    wanted = asked[...].reshape(slot_count, LANES)
    lane = lax.broadcasted_iota(jnp.int32, (slot_count, LANES), 1)
    chosen = jnp.concatenate(
        [jnp.where(wanted == lane + first, 1.0, 0.0) for first in range(0, row_count, LANES)], axis=1
    ).astype(jnp.bfloat16)

    @pl.loop(0, width // TILE)
    def _(step):
        cols = pl.ds(pl.multiple_of(step * TILE, TILE), TILE)
        rows_out[:, :, cols] = (
            jnp.dot(chosen, features[:, cols], preferred_element_type=jnp.float32)
            .astype(jnp.bfloat16)
            .reshape(peers, fetch, TILE)
        )

    for offset in range(1, peers):
        peer = at_offset(offset)
        send(rows_out.at[peer], rows_in.at[me], rows_sems.at[offset], (graph, peer))
    rows_in[pl.ds(me, 1)] = rows_out[pl.ds(me, 1)]
    for part in (2, 3):
        for bit in bits:
            send_on(0, part, bit)

    loads[3].wait()
    loads[4].wait()
    block = 64

    @pl.loop(0, row_count // block)
    def _(step):
        rows = pl.ds(pl.multiple_of(step * block, block), block)
        raw = importance[rows, :]
        scaled = raw / jnp.sum(raw, axis=1, keepdims=True)
        places = slots[rows, :]
        ids = lax.broadcasted_iota(jnp.int32, (block, slot_count), 1)
        mix = jnp.zeros((block, slot_count), jnp.float32)
        for k in range(raw.shape[1]):
            mix = mix + jnp.where(places[:, k : k + 1] == ids, scaled[:, k : k + 1], 0.0)
        mixing[rows, :] = mix.astype(jnp.bfloat16)

    offsets = even_offsets(peers)
    single = [d for d in offsets if d in bits]
    several = [d for d in offsets if d not in bits]
    for d in single:
        relay(d, 0)
        relay(d, 1)

    loads[5].wait()
    loads[6].wait()

    @pl.loop(0, width // TILE)
    def _(step):
        cols = pl.ds(pl.multiple_of(step * TILE, TILE), TILE)
        hidden[:, cols] = (
            jnp.dot(features[...], w_self[:, cols], preferred_element_type=jnp.float32) + z_bias[:, cols]
        )

    loads[7].wait()
    loads[8].wait()
    for offset in range(1, peers):
        await_arrival(rows_in.at[at_offset(offset)], rows_sems.at[offset])

    @pl.loop(0, width // TILE)
    def _(step):
        cols = pl.ds(pl.multiple_of(step * TILE, TILE), TILE)
        message = jnp.maximum(
            jnp.dot(
                rows_in[...].reshape(slot_count, width),
                q_weight[:, cols],
                preferred_element_type=jnp.float32,
            )
            + q_bias[:, cols],
            0.0,
        ).astype(jnp.bfloat16)
        pooled[:, cols] = jnp.dot(mixing[...], message, preferred_element_type=jnp.float32).astype(
            jnp.bfloat16
        )

    for d in single:
        relay(d, 2)
        relay(d, 3)
    loads[9].wait()
    squares[...] = jnp.zeros_like(squares)

    @pl.loop(0, width // TILE)
    def _(step):
        cols = pl.ds(pl.multiple_of(step * TILE, TILE), TILE)
        part = jnp.maximum(
            hidden[:, cols] + jnp.dot(pooled[...], w_neigh[:, cols], preferred_element_type=jnp.float32),
            0.0,
        )
        hidden[:, cols] = part
        for first in range(0, TILE, LANES):
            piece = part[:, first : first + LANES]
            squares[...] += piece * piece

    inverse = lax.rsqrt(jnp.sum(squares[...], axis=1, keepdims=True) / width + 1e-06)
    normed[...] = (hidden[...] * inverse).astype(jnp.bfloat16)

    for part in (0, 1, 2, 3):
        for d in several:
            relay(d, part)

    loads[10].wait()

    def score(offset):
        shard = at_offset(offset)
        scores = lax.dot_general(
            normed[...], shards[shard], (((1,), (1,)), ((), ())), preferred_element_type=jnp.float32
        )
        total[...] = scores if offset == 0 else jnp.where(labels[...] == shard, scores, total[...])

    score(0)
    await_arrival(shards.at[at_offset(1)], side_sems.at[0, 0])
    score(1)
    for d in offsets:
        relay(d, 4)
        relay(d, 5)
        score(d)
    for d in offsets:
        for part in range(6):
            ref = part_ref(d ^ 1, part)
            await_arrival(ref, side_sems.at[d // 2, part])
        score(d ^ 1)
    out_ref[...] = total[...].astype(out_ref.dtype)
    for copy in sent:
        copy.wait_send()


def body(
    graphs,
    peers,
    features,
    q_weight,
    q_bias,
    w_self,
    w_neigh,
    z_bias,
    centroids,
    requests,
    slots,
    importance,
    labels,
):
    rows, width = features.shape
    cents = centroids.shape[0]
    fetch = requests.shape[2]
    slot_count = peers * fetch
    wide = jnp.broadcast_to(requests[0][:, :, None], (peers, fetch, LANES))
    far = peers // 2 - 1
    sends = 12 * far + len(chip_bits(peers)) * 4 + 1 + 2 * (peers - 1)
    bf16, f32, i32 = jnp.bfloat16, jnp.float32, jnp.int32
    dma = pltpu.SemaphoreType.DMA
    flops = 2 * rows * width * (3 * width + peers * cents)
    return pl.pallas_call(
        functools.partial(kernel, graphs, peers),
        out_shape=jax.ShapeDtypeStruct((rows, cents), bf16),
        in_specs=[pl.BlockSpec(memory_space=pl.ANY)] * 11,
        out_specs=pl.BlockSpec(memory_space=pltpu.VMEM),
        scratch_shapes=[
            pltpu.VMEM((rows, width), bf16),
            pltpu.VMEM((width, width), bf16),
            pltpu.VMEM((1, width), f32),
            pltpu.VMEM((width, width), bf16),
            pltpu.VMEM((width, width), bf16),
            pltpu.VMEM((1, width), f32),
            pltpu.VMEM((peers, cents, width), bf16),
            pltpu.VMEM((peers, fetch, LANES), i32),
            pltpu.VMEM(slots.shape, i32),
            pltpu.VMEM(importance.shape, f32),
            pltpu.VMEM(labels.shape, i32),
            pltpu.VMEM((peers, fetch, LANES), i32),
            pltpu.VMEM((peers, fetch, width), bf16),
            pltpu.VMEM((peers, fetch, width), bf16),
            pltpu.VMEM((rows, slot_count), bf16),
            pltpu.VMEM((rows, width), bf16),
            pltpu.VMEM((rows, width), f32),
            pltpu.VMEM((rows, LANES), f32),
            pltpu.VMEM((rows, width), bf16),
            pltpu.VMEM((rows, cents), f32),
            dma((11,)),
            dma((sends,)),
            dma((peers // 2, 6)),
            dma((peers // 2, 6)),
            dma((peers,)),
            dma((peers,)),
        ],
        compiler_params=pltpu.CompilerParams(
            collective_id=0, has_side_effects=True, vmem_limit_bytes=48 * 1024 * 1024
        ),
        cost_estimate=pl.CostEstimate(flops=flops, bytes_accessed=8 * 1024 * 1024, transcendentals=rows),
    )(
        features,
        q_weight,
        q_bias.reshape(1, -1),
        w_self,
        w_neigh,
        z_bias.reshape(1, -1),
        centroids,
        wide,
        slots,
        importance,
        labels,
    )


def solution(mesh):
    return jax.shard_map(
        functools.partial(body, mesh.shape["graph"], mesh.shape["index"]),
        mesh=mesh,
        in_specs=(
            P(("graph", "index"), None),
            P(),
            P(),
            P(),
            P(),
            P(),
            P("index", None),
            P(("graph", "index"), None, None),
            P(("graph", "index"), None),
            P(("graph", "index"), None),
            P(("graph", "index"), None),
        ),
        out_specs=P(("graph", "index"), None),
        check_vma=False,
    )
```

time: 98.2 us -> 39.8 us (0.41)
  waiting for transfers between devices: 37.1 us -> 0 us
  Pallas kernels: 0 us -> 28.5 us
  blocking collectives: 18 us -> 0 us
  matrix products: 14.3 us -> 0 us
  between operations: 13.5 us -> 0.03 us
  other arithmetic: 9.79 us -> 0 us
  local copies, waits for them, and re-layouts: 1.63 us -> 10.7 us
  starting transfers between devices: 3.45 us -> 0 us
    all_gather x1 -> x0, waiting for transfers between devices: 30.2 us -> none  [body(): shard_rows = lax.all_gather(messages, 'index', axis=0, tiled=True)]
    pallas_call x0 -> x1, Pallas kernels: none -> 28.5 us  [body(): pl.pallas_call(functools.partial(kernel, graphs, peers), out_shape=jax.Sh...]
    all_to_all x1 -> x0, blocking collectives: 18 us -> none  [body(): lax.all_to_all(outgoing, 'index', split_axis=0, concat_axis=0, tiled=True)]
    dot_general x5 -> x0, matrix products: 14.3 us -> none  [the longest x1 4.59 us: body(): jnp.dot(local_mix, shard_rows, preferred_element_type=jnp.float32)]
    unnamed x14 -> x16, local copies, waits for them, and re-layouts: 0.03 us -> 9.95 us
    all_to_all x1 -> x0, waiting for transfers between devices: 6.85 us -> none  [body(): lax.all_to_all(raw_scores.reshape(peer_count, arrived.shape[1], cent_coun...]
    reduce_sum x3 -> x0, other arithmetic: 5.68 us -> none  [the longest x1 5.56 us: body(): jnp.sum(jnp.where(slots[:, :, None] == slot_ids[None, None, :], weights_n...]
    all_to_all x1 -> x0, starting transfers between devices: 3.41 us -> none  [body(): lax.all_to_all(raw_scores.reshape(peer_count, arrived.shape[1], cent_coun...]
  transfers between devices with their start and end apart: 2 -> 0, of which waited for: 2 -> 0; matrix products, arithmetic and copies ran while one was open for 9% -> 0% of each run, Pallas kernels for 0% -> 0%
where the time goes in v1:
time: 39.8 us; the launch traced here: 39.3 us
  Pallas kernels  28.5 us (72%)
  local copies, waits for them, and re-layouts  10.7 us (27%)
    pallas_call x1, Pallas kernels, body(): pl.pallas_call(functools.partial(kernel, graphs, peers), out_shape=jax.Sh...  28.5 us
    unnamed x16, local copies, waits for them, and re-layouts  9.95 us

profile of v1, /device:TPU:0, one launch (start us, length us, event | category | flops | bytes accessed | tf_op | source)
XLA Modules:
  0.0 39.3 jit_solution(564427737846013398)
XLA Ops:
  0.0 0.8 %broadcast_in_dim.8.requests_hbm = s32[8,16,128]{2,1,0:T(8,128)S(1)} broadcast(s32[8,16]{1,0:T(8,128)} %bitcast.5), dimensions={0,1} | broadcast | bytes 66048 | tf_op jit(solution)/shard_map/broadcast_in_dim | solution.py:336
  0.8 0.9 %copy.12.slots_hbm = s32[256,50]{1,0:T(8,128)S(1)} copy(s32[256,50]{0,1:T(8,128)} %param.19) | data formatting | bytes 102400 | tf_op args[8]
  1.7 0.9 %copy.13.importance_hbm = f32[256,50]{1,0:T(8,128)S(1)} copy(f32[256,50]{0,1:T(8,128)} %param.20) | data formatting | bytes 102400 | tf_op args[9]
  2.6 0.8 %copy.14.labels_hbm = s32[256,1]{1,0:T(8,128)S(1)} copy(s32[256,1]{0,1:T(1,128)} %param.21) | data formatting | bytes 2048 | tf_op args[10]
  3.4 0.0 copy-start
  3.4 1.6 %copy-done = bf16[1024,1024]{1,0:T(8,128)(2,1)S(1)} copy-done((bf16[1024,1024]{1,0:T(8,128)(2,1)S(1)}, bf16[1024,1024]{1,0:T(8,128)(2,1)}, u32[]{:S(2)}) %copy-start) | copy-done | bytes 2097176
  5.0 0.0 copy-start.1
  5.0 1.6 %copy-done.1 = bf16[1024,1024]{1,0:T(8,128)(2,1)S(1)} copy-done((bf16[1024,1024]{1,0:T(8,128)(2,1)S(1)}, bf16[1024,1024]{1,0:T(8,128)(2,1)}, u32[]{:S(2)}) %copy-start.1) | copy-done | bytes 2097176
  6.6 0.0 copy-start.2
  6.6 1.0 %copy-done.2 = bf16[256,1024]{1,0:T(8,128)(2,1)S(1)} copy-done((bf16[256,1024]{1,0:T(8,128)(2,1)S(1)}, bf16[256,1024]{1,0:T(8,128)(2,1)}, u32[]{:S(2)}) %copy-start.2) | copy-done | bytes 524312
  7.7 0.0 copy-start.3
  7.7 1.0 %copy-done.3 = bf16[256,1024]{1,0:T(8,128)(2,1)S(1)} copy-done((bf16[256,1024]{1,0:T(8,128)(2,1)S(1)}, bf16[256,1024]{1,0:T(8,128)(2,1)}, u32[]{:S(2)}) %copy-start.3) | copy-done | bytes 524312
  8.7 0.0 copy-start.4
  8.7 0.7 %copy-done.4 = f32[1024]{0:T(1024)S(1)} copy-done((f32[1024]{0:T(1024)S(1)}, f32[1024]{0:T(1024)}, u32[]{:S(2)}) %copy-start.4) | copy-done | bytes 4120
  9.4 0.0 copy-start.5
  9.4 0.7 %copy-done.5 = f32[1024]{0:T(1024)S(1)} copy-done((f32[1024]{0:T(1024)S(1)}, f32[1024]{0:T(1024)}, u32[]{:S(2)}) %copy-start.5) | copy-done | bytes 4120
  10.1 28.5 %shard_map.109 = bf16[256,256]{1,0:T(8,128)(2,1)S(1)} custom-call(bf16[256,1024]{1,0:T(8,128)(2,1)S(1)} %copy-done.2, bf16[1024,1024]{1,0:T(8,128)(2,1)S(1)} %copy-done, f32[1,1024]{1,0:T(1,128)S(1)} %bitcast.3, bf16[1024,1024]{1,0:T(8,128)(2,1)S(1)} %copy-done.1, bf16[1024,1024]{1,0:T(8,128)(2,1)} %w_neigh_hbm.1, f32[1,1024]{1,0:T(1,128)S(1)} %bitcast.4, ...), custom_call_target="tpu_custom_call" | custom-call | flops 2684354560 | bytes 8388608 | tf_op jit(solution)/shard_map/pallas_call | solution.py:342
  38.6 0.7 %copy.16 = bf16[256,256]{1,0:T(8,128)(2,1)} copy(bf16[256,256]{1,0:T(8,128)(2,1)S(1)} %shard_map.109) | data formatting | bytes 262144
Async XLA Ops:
  3.4 1.6 %copy-start = (bf16[1024,1024]{1,0:T(8,128)(2,1)S(1)}, bf16[1024,1024]{1,0:T(8,128)(2,1)}, u32[]{:S(2)}) copy-start(bf16[1024,1024]{1,0:T(8,128)(2,1)} %q_weight_hbm.1) | copy-start | bytes 6291460
  5.0 1.6 %copy-start.1 = (bf16[1024,1024]{1,0:T(8,128)(2,1)S(1)}, bf16[1024,1024]{1,0:T(8,128)(2,1)}, u32[]{:S(2)}) copy-start(bf16[1024,1024]{1,0:T(8,128)(2,1)} %w_self_hbm.1) | copy-start | bytes 6291460
  6.6 1.0 %copy-start.2 = (bf16[256,1024]{1,0:T(8,128)(2,1)S(1)}, bf16[256,1024]{1,0:T(8,128)(2,1)}, u32[]{:S(2)}) copy-start(bf16[256,1024]{1,0:T(8,128)(2,1)} %features_hbm.1) | copy-start | bytes 1572868
  7.7 1.0 %copy-start.3 = (bf16[256,1024]{1,0:T(8,128)(2,1)S(1)}, bf16[256,1024]{1,0:T(8,128)(2,1)}, u32[]{:S(2)}) copy-start(bf16[256,1024]{1,0:T(8,128)(2,1)} %centroids_hbm.1) | copy-start | bytes 1572868
  8.7 0.7 %copy-start.4 = (f32[1024]{0:T(1024)S(1)}, f32[1024]{0:T(1024)}, u32[]{:S(2)}) copy-start(f32[1024]{0:T(1024)} %param.13) | copy-start | bytes 12292
  9.4 0.7 %copy-start.5 = (f32[1024]{0:T(1024)S(1)}, f32[1024]{0:T(1024)}, u32[]{:S(2)}) copy-start(f32[1024]{0:T(1024)} %param.16) | copy-start | bytes 12292

commit v2 on v1

--- a/solution.py
+++ b/solution.py
@@ -46,6 +46,7 @@
     slots,
     importance,
     labels,
+    label_rows,
     asked,
     rows_out,
     rows_in,
@@ -66,7 +67,7 @@
     me = lax.axis_index("index")
     row_count, width = features.shape
     cents = shards.shape[1]
-    fetch = requests.shape[1]
+    fetch = rows_in.shape[1]
     slot_count = peers * fetch
     bits = chip_bits(peers)
 
@@ -174,8 +175,8 @@
     loads[0].wait()
     for offset in range(1, peers):
         peer = at_offset(offset)
-        send(requests.at[peer], asked.at[me], asked_sems.at[offset], (graph, peer))
-    asked[pl.ds(me, 1)] = requests[pl.ds(me, 1)]
+        send(requests, asked.at[me], asked_sems.at[offset], (graph, peer))
+    asked[pl.ds(me, 1)] = requests[...][None]
 
     loads[2].wait()
     for part in (0, 1):
@@ -186,11 +187,14 @@
     loads[1].wait()
     for offset in range(1, peers):
         await_arrival(asked.at[at_offset(offset)], asked_sems.at[offset])
-    wanted = asked[...].reshape(slot_count, LANES)
-    lane = lax.broadcasted_iota(jnp.int32, (slot_count, LANES), 1)
-    chosen = jnp.concatenate(
-        [jnp.where(wanted == lane + first, 1.0, 0.0) for first in range(0, row_count, LANES)], axis=1
-    ).astype(jnp.bfloat16)
+    lists = jnp.concatenate(
+        [jnp.broadcast_to(asked[p, pl.ds(me, 1), :], (fetch, fetch)) for p in range(peers)], axis=0
+    )
+    own = lax.broadcasted_iota(jnp.int32, (slot_count, fetch), 0) % fetch
+    turn = lax.broadcasted_iota(jnp.int32, (slot_count, fetch), 1)
+    wanted = jnp.sum(jnp.where(own == turn, lists, 0).astype(jnp.float32), axis=1, keepdims=True)
+    ids = lax.broadcasted_iota(jnp.int32, (slot_count, row_count), 1).astype(jnp.float32)
+    chosen = jnp.where(wanted == ids, 1.0, 0.0).astype(jnp.bfloat16)
 
     @pl.loop(0, width // TILE)
     def _(step):
@@ -211,19 +215,19 @@
 
     loads[3].wait()
     loads[4].wait()
-    block = 64
+    block = 128
 
     @pl.loop(0, row_count // block)
     def _(step):
         rows = pl.ds(pl.multiple_of(step * block, block), block)
-        raw = importance[rows, :]
-        scaled = raw / jnp.sum(raw, axis=1, keepdims=True)
-        places = slots[rows, :]
-        ids = lax.broadcasted_iota(jnp.int32, (block, slot_count), 1)
-        mix = jnp.zeros((block, slot_count), jnp.float32)
-        for k in range(raw.shape[1]):
-            mix = mix + jnp.where(places[:, k : k + 1] == ids, scaled[:, k : k + 1], 0.0)
-        mixing[rows, :] = mix.astype(jnp.bfloat16)
+        scaled = importance[:, rows] / jnp.sum(importance[:, rows], axis=0, keepdims=True)
+        places = slots[:, rows]
+        for first in range(0, slot_count, LANES):
+            ids = lax.broadcasted_iota(jnp.int32, (LANES, block), 0) + first
+            mix = jnp.zeros((LANES, block), jnp.float32)
+            for k in range(places.shape[0]):
+                mix = mix + jnp.where(places[k : k + 1, :] == ids, scaled[k : k + 1, :], 0.0)
+            mixing[rows, first : first + LANES] = mix.T.astype(jnp.bfloat16)
 
     offsets = even_offsets(peers)
     single = [d for d in offsets if d in bits]
@@ -289,13 +293,16 @@
             relay(d, part)
 
     loads[10].wait()
+    label_rows[...] = jnp.broadcast_to(labels[...], (LANES, row_count)).T
 
     def score(offset):
         shard = at_offset(offset)
         scores = lax.dot_general(
             normed[...], shards[shard], (((1,), (1,)), ((), ())), preferred_element_type=jnp.float32
         )
-        total[...] = scores if offset == 0 else jnp.where(labels[...] == shard, scores, total[...])
+        total[...] = scores if offset == 0 else jnp.where(
+            jnp.concatenate([label_rows[...]] * (cents // LANES), axis=1) == shard, scores, total[...]
+        )
 
     score(0)
     await_arrival(shards.at[at_offset(1)], side_sems.at[0, 0])
@@ -333,7 +340,6 @@
     cents = centroids.shape[0]
     fetch = requests.shape[2]
     slot_count = peers * fetch
-    wide = jnp.broadcast_to(requests[0][:, :, None], (peers, fetch, LANES))
     far = peers // 2 - 1
     sends = 12 * far + len(chip_bits(peers)) * 4 + 1 + 2 * (peers - 1)
     bf16, f32, i32 = jnp.bfloat16, jnp.float32, jnp.int32
@@ -342,7 +348,7 @@
     return pl.pallas_call(
         functools.partial(kernel, graphs, peers),
         out_shape=jax.ShapeDtypeStruct((rows, cents), bf16),
-        in_specs=[pl.BlockSpec(memory_space=pl.ANY)] * 11,
+        in_specs=[pl.BlockSpec(memory_space=pltpu.HBM)] * 11,
         out_specs=pl.BlockSpec(memory_space=pltpu.VMEM),
         scratch_shapes=[
             pltpu.VMEM((rows, width), bf16),
@@ -352,11 +358,12 @@
             pltpu.VMEM((width, width), bf16),
             pltpu.VMEM((1, width), f32),
             pltpu.VMEM((peers, cents, width), bf16),
-            pltpu.VMEM((peers, fetch, LANES), i32),
-            pltpu.VMEM(slots.shape, i32),
-            pltpu.VMEM(importance.shape, f32),
-            pltpu.VMEM(labels.shape, i32),
-            pltpu.VMEM((peers, fetch, LANES), i32),
+            pltpu.VMEM((peers, fetch), i32),
+            pltpu.VMEM(slots.shape[::-1], i32),
+            pltpu.VMEM(importance.shape[::-1], f32),
+            pltpu.VMEM((1, rows), i32),
+            pltpu.VMEM((rows, LANES), i32),
+            pltpu.VMEM((peers, peers, fetch), i32),
             pltpu.VMEM((peers, fetch, width), bf16),
             pltpu.VMEM((peers, fetch, width), bf16),
             pltpu.VMEM((rows, slot_count), bf16),
@@ -373,7 +380,7 @@
             dma((peers,)),
         ],
         compiler_params=pltpu.CompilerParams(
-            collective_id=0, has_side_effects=True, vmem_limit_bytes=48 * 1024 * 1024
+            collective_id=0, has_side_effects=True, vmem_limit_bytes=58 * 1024 * 1024
         ),
         cost_estimate=pl.CostEstimate(flops=flops, bytes_accessed=8 * 1024 * 1024, transcendentals=rows),
     )(
@@ -384,10 +391,10 @@
         w_neigh,
         z_bias.reshape(1, -1),
         centroids,
-        wide,
-        slots,
-        importance,
-        labels,
+        requests[0],
+        slots.T,
+        importance.T,
+        labels.reshape(1, -1),
     )
 
 

time: 39.8 us -> 29.6 us (0.74)
  local copies, waits for them, and re-layouts: 10.7 us -> 1.57 us
  Pallas kernels: 28.5 us -> 27.9 us
    unnamed x16 -> x1, local copies, waits for them, and re-layouts: 9.95 us -> 1.57 us
    broadcast_in_dim x1 -> x0, local copies, waits for them, and re-layouts: 0.76 us -> none  [body(): wide = jnp.broadcast_to(requests[0][:, :, None], (peers, fetch, LANES))]
    pallas_call x1, Pallas kernels: 28.5 us -> 27.9 us  [body(): pl.pallas_call(functools.partial(kernel, graphs, peers), out_shape=jax.Sh...]
where the time goes in v2:
time: 29.6 us; the launch traced here: 29.4 us
  Pallas kernels  27.9 us (94%)
  local copies, waits for them, and re-layouts  1.57 us (5%)
    pallas_call x1, Pallas kernels, body(): pl.pallas_call(functools.partial(kernel, graphs, peers), out_shape=jax.Sh...  27.9 us
    unnamed x1, local copies, waits for them, and re-layouts  1.57 us

profile of v2, /device:TPU:0, one launch (start us, length us, event | category | flops | bytes accessed | tf_op | source)
XLA Modules:
  0.0 29.4 jit_solution(16728469552552388578)
XLA Ops:
  0.0 27.9 %shard_map.109 = bf16[256,256]{1,0:T(8,128)(2,1)} custom-call(bf16[256,1024]{1,0:T(8,128)(2,1)} %features_hbm.1, bf16[1024,1024]{1,0:T(8,128)(2,1)} %q_weight_hbm.1, f32[1,1024]{1,0:T(1,128)} %bitcast.8, bf16[1024,1024]{1,0:T(8,128)(2,1)} %w_self_hbm.1, bf16[1024,1024]{1,0:T(8,128)(2,1)} %w_neigh_hbm.1, f32[1,1024]{1,0:T(1,128)} %bitcast.9, ...), custom_call_target="tpu_custom_call" | custom-call | flops 2684354560 | bytes 8388608 | tf_op jit(solution)/shard_map/pallas_call | solution.py:348
  27.9 1.6 %copy.13 = bf16[256,256]{1,0:T(8,128)(2,1)} copy(bf16[256,256]{1,0:T(8,128)(2,1)} %shard_map.109) | data formatting | bytes 262144

commit v3 on v2

--- a/solution.py
+++ b/solution.py
@@ -10,6 +10,7 @@
 MESH = pl.DeviceIdType.MESH
 LANES = 128
 TILE = 256
+CHUNKS = 2
 
 
 def chip_bits(peers):
@@ -86,21 +87,19 @@
     role = graph % 2
     across = flip(graph, 1)
 
-    share = cents * 5 // 16 // 16 * 16
-    common = cents - 2 * share
-    share_a = (share // 2 + 15) // 16 * 16
-    common_a = (common // 2 + 15) // 16 * 16
+    half = cents // 2
+    size = half // CHUNKS
+    top = bits[-1]
 
     def rows_of(part):
-        start, size = {
-            0: (role * share, share_a),
-            1: (role * share + share_a, share - share_a),
-            2: (2 * share, common_a),
-            3: (2 * share + common_a, common - common_a),
-            4: ((1 - role) * share, share_a),
-            5: ((1 - role) * share + share_a, share - share_a),
-        }[part]
-        return pl.ds(start if isinstance(start, int) else pl.multiple_of(start, 16), size)
+        first = role if part < CHUNKS else 1 - role
+        return pl.ds(pl.multiple_of(first * half + part % CHUNKS * size, 16), size)
+
+    def onward(offset, part):
+        if part < CHUNKS:
+            return [bit for bit in bits if bit > offset and offset | bit != top]
+        low = offset & -offset if offset else 2 * top
+        return [bit for bit in bits if bit < low and offset | bit != bits[0]]
 
     loads = []
     for source, target in (
@@ -160,16 +159,11 @@
     def relay(offset, part):
         ref = part_ref(offset, part)
         await_arrival(ref, main_sems.at[offset // 2, part])
-        if part in (0, 2):
-            for bit in bits:
-                if bit > offset:
-                    send_on(offset, part, bit)
-        elif part in (1, 3):
-            for bit in bits:
-                if bit < (offset & -offset):
-                    send_on(offset, part, bit)
-        if part in (0, 1):
-            send(ref, ref, main_sems.at[offset // 2, part + 4], (across, me))
+        for bit in onward(offset, part):
+            send_on(offset, part, bit)
+        if (offset == bits[0] and part < CHUNKS) or (offset == top and part >= CHUNKS):
+            other = (part + CHUNKS) % (2 * CHUNKS)
+            send(ref, ref, main_sems.at[offset // 2, other], (across, me))
         send(ref, ref, side_sems.at[offset // 2, part], (graph, flip(me, 1)))
 
     loads[0].wait()
@@ -179,10 +173,45 @@
     asked[pl.ds(me, 1)] = requests[...][None]
 
     loads[2].wait()
-    for part in (0, 1):
-        for bit in bits:
-            send_on(0, part, bit)
+    for chunk in range(CHUNKS):
+        for part in (chunk, chunk + CHUNKS):
+            for bit in onward(0, part):
+                send_on(0, part, bit)
     send(shards.at[me], shards.at[me], side_sems.at[0, 0], (graph, flip(me, 1)))
+
+    loads[3].wait()
+    loads[4].wait()
+    block = 128
+
+    @pl.loop(0, row_count // block)
+    def _(step):
+        rows = pl.ds(pl.multiple_of(step * block, block), block)
+        scaled = importance[:, rows] / jnp.sum(importance[:, rows], axis=0, keepdims=True)
+        places = slots[:, rows]
+        for first in range(0, slot_count, LANES):
+            ids = lax.broadcasted_iota(jnp.int32, (LANES, block), 0) + first
+            mix = jnp.zeros((LANES, block), jnp.float32)
+            for k in range(places.shape[0]):
+                mix = mix + jnp.where(places[k : k + 1, :] == ids, scaled[k : k + 1, :], 0.0)
+            mixing[rows, first : first + LANES] = mix.T.astype(jnp.bfloat16)
+
+    by_tree = [(d, part) for d in even_offsets(peers) for part in range(2 * CHUNKS)]
+    by_layer = [(bits[0], part + CHUNKS) for part in range(CHUNKS)] + [(top, part) for part in range(CHUNKS)]
+    by_tree = [event for event in by_tree if event not in by_layer]
+    rounds = []
+    for late in (False, True):
+        for chunk in range(CHUNKS):
+            events = [e for e in by_tree if (e[0] not in bits) == late and e[1] % CHUNKS == chunk]
+            events += [e for e in by_layer if late and e[1] % CHUNKS == chunk]
+            rounds.append(events)
+
+    def relay_rounds(count):
+        for events in rounds[:count]:
+            for offset, part in events:
+                relay(offset, part)
+        del rounds[:count]
+
+    relay_rounds(CHUNKS // 2)
 
     loads[1].wait()
     for offset in range(1, peers):
@@ -209,32 +238,8 @@
         peer = at_offset(offset)
         send(rows_out.at[peer], rows_in.at[me], rows_sems.at[offset], (graph, peer))
     rows_in[pl.ds(me, 1)] = rows_out[pl.ds(me, 1)]
-    for part in (2, 3):
-        for bit in bits:
-            send_on(0, part, bit)
-
-    loads[3].wait()
-    loads[4].wait()
-    block = 128
-
-    @pl.loop(0, row_count // block)
-    def _(step):
-        rows = pl.ds(pl.multiple_of(step * block, block), block)
-        scaled = importance[:, rows] / jnp.sum(importance[:, rows], axis=0, keepdims=True)
-        places = slots[:, rows]
-        for first in range(0, slot_count, LANES):
-            ids = lax.broadcasted_iota(jnp.int32, (LANES, block), 0) + first
-            mix = jnp.zeros((LANES, block), jnp.float32)
-            for k in range(places.shape[0]):
-                mix = mix + jnp.where(places[k : k + 1, :] == ids, scaled[k : k + 1, :], 0.0)
-            mixing[rows, first : first + LANES] = mix.T.astype(jnp.bfloat16)
-
-    offsets = even_offsets(peers)
-    single = [d for d in offsets if d in bits]
-    several = [d for d in offsets if d not in bits]
-    for d in single:
-        relay(d, 0)
-        relay(d, 1)
+
+    relay_rounds(CHUNKS // 2)
 
     loads[5].wait()
     loads[6].wait()
@@ -267,9 +272,7 @@
             jnp.bfloat16
         )
 
-    for d in single:
-        relay(d, 2)
-        relay(d, 3)
+    relay_rounds(CHUNKS // 2)
     loads[9].wait()
     squares[...] = jnp.zeros_like(squares)
 
@@ -288,33 +291,57 @@
     inverse = lax.rsqrt(jnp.sum(squares[...], axis=1, keepdims=True) / width + 1e-06)
     normed[...] = (hidden[...] * inverse).astype(jnp.bfloat16)
 
-    for part in (0, 1, 2, 3):
-        for d in several:
-            relay(d, part)
-
     loads[10].wait()
     label_rows[...] = jnp.broadcast_to(labels[...], (LANES, row_count)).T
+    same = jnp.concatenate([label_rows[...]] * (half // LANES), axis=1)
+
+    def dots(block):
+        return lax.dot_general(
+            normed[...], block, (((1,), (1,)), ((), ())), preferred_element_type=jnp.float32
+        )
 
     def score(offset):
         shard = at_offset(offset)
-        scores = lax.dot_general(
-            normed[...], shards[shard], (((1,), (1,)), ((), ())), preferred_element_type=jnp.float32
-        )
-        total[...] = scores if offset == 0 else jnp.where(
-            jnp.concatenate([label_rows[...]] * (cents // LANES), axis=1) == shard, scores, total[...]
-        )
-
+        scores = dots(shards[shard])
+        if offset == 0:
+            total[...] = scores
+        else:
+            total[...] = jnp.where(jnp.concatenate([same, same], axis=1) == shard, scores, total[...])
+
+    def score_halves(low, high, first):
+        parts = ((at_offset(low), first), (at_offset(high), 1 - first))
+        spans = [pl.ds(pl.multiple_of(which * half, half), half) for _, which in parts]
+        scores = dots(
+            jnp.concatenate([shards[shard, span, :] for (shard, _), span in zip(parts, spans)], axis=0)
+        )
+        for place, ((shard, _), span) in enumerate(zip(parts, spans)):
+            piece = scores[:, place * half : (place + 1) * half]
+            total[:, span] = jnp.where(same == shard, piece, total[:, span])
+
+    def await_side(offset, parts):
+        for part in parts:
+            await_arrival(part_ref(offset ^ 1, part), side_sems.at[offset // 2, part])
+
+    ahead, behind = range(CHUNKS), range(CHUNKS, 2 * CHUNKS)
+    relay_rounds(CHUNKS // 2)
     score(0)
     await_arrival(shards.at[at_offset(1)], side_sems.at[0, 0])
     score(1)
-    for d in offsets:
-        relay(d, 4)
-        relay(d, 5)
+    relay_rounds(CHUNKS // 4)
+    score_halves(bits[0], top, role)
+    await_side(bits[0], ahead)
+    await_side(top, behind)
+    score_halves(bits[0] ^ 1, top ^ 1, role)
+    relay_rounds(2 * CHUNKS)
+    score_halves(bits[0], top, 1 - role)
+    others = [d for d in even_offsets(peers) if d not in (bits[0], top)]
+    for d in others:
         score(d)
-    for d in offsets:
-        for part in range(6):
-            ref = part_ref(d ^ 1, part)
-            await_arrival(ref, side_sems.at[d // 2, part])
+    await_side(bits[0], behind)
+    await_side(top, ahead)
+    score_halves(bits[0] ^ 1, top ^ 1, 1 - role)
+    for d in others:
+        await_side(d, range(2 * CHUNKS))
         score(d ^ 1)
     out_ref[...] = total[...].astype(out_ref.dtype)
     for copy in sent:
@@ -341,7 +368,7 @@
     fetch = requests.shape[2]
     slot_count = peers * fetch
     far = peers // 2 - 1
-    sends = 12 * far + len(chip_bits(peers)) * 4 + 1 + 2 * (peers - 1)
+    sends = 4 * CHUNKS * far + 1 + 2 * (peers - 1)
     bf16, f32, i32 = jnp.bfloat16, jnp.float32, jnp.int32
     dma = pltpu.SemaphoreType.DMA
     flops = 2 * rows * width * (3 * width + peers * cents)
@@ -374,8 +401,8 @@
             pltpu.VMEM((rows, cents), f32),
             dma((11,)),
             dma((sends,)),
-            dma((peers // 2, 6)),
-            dma((peers // 2, 6)),
+            dma((peers // 2, 2 * CHUNKS)),
+            dma((peers // 2, 2 * CHUNKS)),
             dma((peers,)),
             dma((peers,)),
         ],

time: 29.6 us -> 28 us (0.946)
  Pallas kernels: 27.9 us -> 26.3 us
    pallas_call x1, Pallas kernels: 27.9 us -> 26.3 us  [body(): pl.pallas_call(functools.partial(kernel, graphs, peers), out_shape=jax.Sh...]
where the time goes in v3:
time: 28 us; the launch traced here: 27.9 us
  Pallas kernels  26.3 us (94%)
  local copies, waits for them, and re-layouts  1.57 us (6%)
    pallas_call x1, Pallas kernels, body(): pl.pallas_call(functools.partial(kernel, graphs, peers), out_shape=jax.Sh...  26.3 us
    unnamed x1, local copies, waits for them, and re-layouts  1.57 us

profile of v3, /device:TPU:0, one launch (start us, length us, event | category | flops | bytes accessed | tf_op | source)
XLA Modules:
  0.0 27.9 jit_solution(7847572688738432219)
XLA Ops:
  0.0 26.3 %shard_map.109 = bf16[256,256]{1,0:T(8,128)(2,1)} custom-call(bf16[256,1024]{1,0:T(8,128)(2,1)} %features_hbm.1, bf16[1024,1024]{1,0:T(8,128)(2,1)} %q_weight_hbm.1, f32[1,1024]{1,0:T(1,128)} %bitcast.8, bf16[1024,1024]{1,0:T(8,128)(2,1)} %w_self_hbm.1, bf16[1024,1024]{1,0:T(8,128)(2,1)} %w_neigh_hbm.1, f32[1,1024]{1,0:T(1,128)} %bitcast.9, ...), custom_call_target="tpu_custom_call" | custom-call | flops 2684354560 | bytes 8388608 | tf_op jit(solution)/shard_map/pallas_call | solution.py:375
  26.3 1.6 %copy.13 = bf16[256,256]{1,0:T(8,128)(2,1)} copy(bf16[256,256]{1,0:T(8,128)(2,1)} %shard_map.109) | data formatting | bytes 262144
